TPU v7x, 256 devices: a whole 4x4x8 slice. The times are simulated.
256 devices in a mesh: tile: 32 (over z, y), lev: 8 (over x, core).
Axes of the slice: x: 4, y: 4, z: 8, core: 2. Of those that a mesh axis runs over, the one named last changes fastest.
Arguments:
- members: bfloat16 [32, 65536, 128], P('lev', 'tile'), may hold values from -4 to 4
- obs_operator: bfloat16 [8, 2048, 4, 128, 128], P('lev', 'tile'), as said below
- col_level: int32 [8, 2048, 4], P('lev', 'tile'), may hold values from 0 to 3
- col_block: int32 [8, 2048, 4], P('lev', 'tile'), may hold values from 0 to 19, as said below
- obs_count: int32 [2048], P(('tile', 'lev')), may hold values from 1 to 128, as said below
- obs_values: float32 [2048, 128], P(('tile', 'lev')), may hold values from -60 to 60
- obs_weight: float32 [2048, 128], P(('tile', 'lev')), may hold values from 0.01 to 0.18
Outputs:
- analysed: bfloat16 [32, 65536, 128], P('lev', 'tile')
- transform: float32 [128, 128], replicated
Inputs may be any that keep to these rules, and one draw needn't show every extreme that they name: `col_block`: for the observation block in position i of its tile (i < 64), every column block lies within 2 of i * 16 // 64 + 2, and never names a block outside the grid. `obs_count`: the first block of every tile uses all 128 rows. `obs_operator`: entries lie within 4 / sqrt(8192) of zero.
All inputs are finite; a program needn't handle non-finite values.
Results may differ from a plain program's by a relative error of at most 0.0076.
Values may be sent and summed in bfloat16 or wider, within the bound.
No kernel may reach another device: no remote copies, remote signals or barrier semaphores. Data moves between devices by JAX's collectives and lax.ppermute only.
A program may use at most 128 MiB of HBM per device.

v0:
```python
import math
import jax
import jax.numpy as jnp
from jax import lax
from jax.sharding import PartitionSpec as P

HALO = 2


def with_halo(value, sides, width):
    for axis, dim in sides:
        count, length = (lax.axis_size(axis), value.shape[dim])
        up = [(i, (i + 1) % count) for i in range(count - 1)]
        down = [(j, i) for i, j in up]
        last = lax.slice_in_dim(value, length - width, length, axis=dim)
        first = lax.slice_in_dim(value, 0, width, axis=dim)
        before = lax.ppermute(last, axis, up)
        after = lax.ppermute(first, axis, down)
        value = jnp.concatenate([before, value, after], axis=dim)
    return value


def shards(members, obs_operator, col_level, col_block, obs_count, obs_values, obs_weight):
    highest = lax.Precision.HIGHEST
    lev_local, cells_local, ensemble = members.shape
    block_size = obs_operator.shape[-1]
    rim_cells = HALO * block_size
    padded = with_halo(members, (("tile", 1),), rim_cells)
    window_blocks = padded.shape[1] // block_size
    column_blocks = padded.reshape(lev_local, window_blocks, block_size, ensemble).reshape(
        lev_local * window_blocks, block_size, ensemble
    )
    operator_blocks = obs_operator[0]
    flat_index = col_level[0] * window_blocks + col_block[0]
    live_rows = (jnp.arange(block_size, dtype=jnp.int32)[None, :] < obs_count[:, None]).astype(
        jnp.float32
    )
    weight_local = obs_weight * live_rows
    chosen = column_blocks[flat_index]
    observed = lax.psum_scatter(
        jnp.einsum("okij,okjm->oim", operator_blocks, chosen, preferred_element_type=jnp.float32),
        "lev",
        scatter_dimension=0,
        tiled=True,
    )
    weight, values_used = (weight_local, obs_values)
    mean_obs = jnp.sum(observed, axis=2) / ensemble
    row_scale = weight / math.sqrt(ensemble - 1)
    spread = ((observed - mean_obs[:, :, None]) * row_scale[:, :, None]).reshape(-1, ensemble)
    innovation = ((values_used - mean_obs) * weight).reshape(-1)
    gram_local = jnp.dot(spread.T, spread, precision=highest, preferred_element_type=jnp.float32)
    pull_local = jnp.dot(innovation, spread, precision=highest, preferred_element_type=jnp.float32)
    identity = jnp.eye(ensemble, dtype=jnp.float32)
    gram, pull = lax.psum((gram_local, pull_local), ("tile", "lev"))
    lower = jnp.linalg.cholesky(identity + gram)
    inverse = lax.linalg.triangular_solve(lower, identity, left_side=True, lower=True)
    shift_weights = jnp.dot(inverse.T, jnp.dot(inverse, pull, precision=highest), precision=highest)
    transform = shift_weights[:, None] / math.sqrt(ensemble - 1) + inverse.T
    transform_bf = transform.astype(jnp.bfloat16)
    row_mean = jnp.sum(members, axis=2, dtype=jnp.float32) / ensemble
    anomalies = (members.astype(jnp.float32) - row_mean[:, :, None]).astype(jnp.bfloat16)
    moved = jnp.dot(
        anomalies.reshape(-1, ensemble), transform_bf, preferred_element_type=jnp.float32
    )
    analysed = (row_mean[:, :, None] + moved.reshape(lev_local, cells_local, ensemble)).astype(
        jnp.bfloat16
    )
    return (analysed, transform)


def solution(mesh):
    placed = (
        P("lev", "tile", None),
        P("lev", "tile", None, None, None),
        P("lev", "tile", None),
        P("lev", "tile", None),
        P(("tile", "lev")),
        P(("tile", "lev"), None),
        P(("tile", "lev"), None),
    )
    return jax.shard_map(
        shards, mesh=mesh, in_specs=placed, out_specs=(P("lev", "tile", None), P()), check_vma=False
    )
```

profile of v0, /device:TPU:1, one launch (start us, length us, event | category | flops | bytes accessed | tf_op | source)
XLA Modules:
  0.0 369.6 jit_solution(11171952963979726350)
XLA Ops:
  7.2 0.0 reduce-scatter.2.cloned.1.call-start
  7.2 1.1 fusion.23
  8.3 4.0 %collective-permute-start = (bf16[4,256,128]{2,1,0:T(8,128)(2,1)S(1)}, bf16[4,256,128]{2,1,0:T(8,128)(2,1)S(1)}, u32[]{:S(2)}, u32[]{:S(2)}) collective-permute-start(bf16[4,256,128]{2,1,0:T(8,128)(2,1)S(1)} %get-tuple-element.6), channel_id=1, source_target_pairs={{0,8},{8,16},{16,24},{24,32},{32,40},{40,48},{48,56},{56,64},{64,7... | collective-permute-start | bytes 786440 | tf_op jit(solution)/shard_map/ppermute | solution.py:17
  12.3 1.3 collective-permute-start.1
  13.6 0.7 compare_select_fusion
  14.3 0.1 copy.14
  14.4 0.1 reshape.63
  14.6 2.7 collective-permute-done
  17.3 3.8 %collective-permute-done.1 = bf16[4,256,128]{2,1,0:T(8,128)(2,1)S(1)} collective-permute-done((bf16[4,256,128]{2,1,0:T(8,128)(2,1)S(1)}, bf16[4,256,128]{2,1,0:T(8,128)(2,1)S(1)}, u32[]{:S(2)}, u32[]{:S(2)}) %collective-permute-start.1) | collective-permute-done | bytes 262176 | tf_op jit(solution)/shard_map/ppermute | solution.py:18
  21.1 1.8 pad_maximum_fusion
  22.9 8.6 %gather_fusion = bf16[256,128,128]{2,1,0:T(8,128)(2,1)} fusion(bf16[80,128,128]{2,1,0:T(8,128)(2,1)S(1)} %bitcast.54, s32[1024]{0:T(1024)S(1)} %pad_clamp_fusion), kind=kCustom, calls=%fused_computation | custom fusion | bytes 16778240 | tf_op jit(solution)/shard_map/gather | solution.py:39
  31.5 10.1 %fusion.3 = f32[64,128,128]{1,2,0:T(8,128)} fusion(bf16[64,4,128,128]{3,2,1,0:T(8,128)(2,1)} %bitcast.55, bf16[1,64,4,128,128]{4,3,2,1,0:T(8,128)(2,1)} %param.8), kind=kOutput, calls=%fused_computation.8 | convolution fusion | flops 1073741824 | bytes 20971520 | tf_op jit(solution)/shard_map/okij,okjm->oim/dot_general | solution.py:41
  41.6 0.0 copy-start
  41.6 0.0 copy-start.1
  41.6 0.0 copy-start.2
  41.6 0.0 copy-start.3
  41.6 0.0 reduce-scatter.2.cloned.1.call-update
  41.7 0.0 all-reduce.2.cloned.1.call-start
  41.7 1.5 copy-done
  43.2 0.6 convert_reduce_fusion
  43.9 41.4 %reduce-scatter.2.cloned.1.call-done = f32[8,128,128]{1,2,0:T(8,128)} async-done(((f32[64,128,128]{1,2,0:T(8,128)}), f32[8,128,128]{1,2,0:T(8,128)}) %reduce-scatter.2.cloned.1.call-update) | async-done | bytes 524304 | tf_op jit(solution)/shard_map/reduce_scatter | solution.py:40
  85.3 1.1 reduce_sum.19
  86.4 0.0 copy-done.1
  86.4 0.0 copy-done.2
  86.4 0.0 copy-done.3
  86.4 0.1 subtract_multiply_fusion.3
  86.5 2.5 convolution_bitcast_fusion
  89.0 0.0 all-reduce.2.cloned.1.call-update
  89.0 1.6 convolution_bitcast_fusion.3
  90.5 79.5 %psum.15 = f32[128]{0:T(128)S(1)} all-reduce(f32[128]{0:T(128)S(1)} %convolution_bitcast_fusion.3), channel_id=1, replica_groups=mesh['tile'=32,'lev'=8] {'tile','lev'}, use_global_device_ids=true, to_apply=%region_6.7 | all-reduce | flops 128 | bytes 1024 | tf_op jit(solution)/shard_map/psum | solution.py:54
  170.0 161.5 %all-reduce.2.cloned.1.call-done = f32[128,128]{1,0:T(8,128)} async-done(((f32[128,128]{1,0:T(8,128)}), f32[128,128]{1,0:T(8,128)}) %all-reduce.2.cloned.1.call-update) | async-done | bytes 65552 | tf_op jit(solution)/shard_map/psum | solution.py:54
  331.5 0.9 convert_add_fusion
  332.3 0.1 copy.17
  332.4 0.9 fusion.17
  333.3 11.7 %cholesky.18 = f32[128,128]{1,0:T(8,128)S(1)} custom-call(f32[128,128]{1,0:T(8,128)S(1)} %fusion.17), custom_call_target="Cholesky" | custom-call | tf_op jit(solution)/shard_map/jit(cholesky)/cholesky | solution.py:55
  345.0 0.6 compare_reduce_fusion
  345.7 0.7 fusion.13
  346.3 9.8 %custom-call.6 = f32[1,128,128]{1,2,0:T(8,128)S(1)} custom-call(f32[1,128,128]{2,1,0:T(8,128)S(1)} %fusion.13), custom_call_target="InvertDiagBlocksLowerTriangular" | custom-call | tf_op jit(solution)/shard_map/triangular_solve | solution.py:56
  356.1 0.2 fusion.15
  356.4 0.2 convolution_bitcast_fusion.2
  356.6 0.2 fusion.8
  356.8 0.7 copy.19
  357.5 5.3 %add_convert_fusion = bf16[4,2048,128]{2,1,0:T(8,128)(2,1)} fusion(bf16[4,2048,128]{2,1,0:T(8,128)(2,1)S(1)} %copy-done, f32[4,2048]{1,0:T(4,128)S(1)} %broadcast_multiply_fusion, f32[128,128]{0,1:T(8,128)S(1)} %bitcast_add_fusion), kind=kOutput, calls=%fused_computation.6 | convolution fusion | flops 273694720 | bytes 4292608 | tf_op jit(solution)/shard_map/dot_general | solution.py:62
  (4 shorter events, 0.1 us)
Async XLA Ops:
  7.2 78.2 %reduce-scatter.2.cloned.1.call-start = ((), (), s32[]{:S(2)}) async-start(), calls=%async_computation.1 | async-start | bytes 4718592 | tf_op jit(solution)/shard_map/reduce_scatter | solution.py:40
  8.3 9.0 %collective-permute-start = (bf16[4,256,128]{2,1,0:T(8,128)(2,1)S(1)}, bf16[4,256,128]{2,1,0:T(8,128)(2,1)S(1)}, u32[]{:S(2)}, u32[]{:S(2)}) collective-permute-start(bf16[4,256,128]{2,1,0:T(8,128)(2,1)S(1)} %get-tuple-element.6), channel_id=1, source_target_pairs={{0,8},{8,16},{16,24},{24,32},{32,40},{40,48},{48,56},{56,64},{64,7... | collective-permute-start | bytes 786440 | tf_op jit(solution)/shard_map/ppermute | solution.py:17
  12.3 8.8 %collective-permute-start.1 = (bf16[4,256,128]{2,1,0:T(8,128)(2,1)S(1)}, bf16[4,256,128]{2,1,0:T(8,128)(2,1)S(1)}, u32[]{:S(2)}, u32[]{:S(2)}) collective-permute-start(bf16[4,256,128]{2,1,0:T(8,128)(2,1)S(1)} %get-tuple-element.7), channel_id=1, source_target_pairs={{8,0},{16,8},{24,16},{32,24},{40,32},{48,40},{56,48},{64,56},{72,6... | collective-permute-start | bytes 786440 | tf_op jit(solution)/shard_map/ppermute | solution.py:18
  41.6 1.6 copy-start
  41.6 44.8 %copy-start.1 = (f32[8,128]{1,0:T(8,128)S(1)}, f32[8,128]{1,0:T(8,128)}, u32[]{:S(2)}) copy-start(f32[8,128]{1,0:T(8,128)} %param.12) | copy-start | bytes 12292
  41.6 44.8 %copy-start.2 = (f32[8,128]{1,0:T(8,128)S(1)}, f32[8,128]{1,0:T(8,128)}, u32[]{:S(2)}) copy-start(f32[8,128]{1,0:T(8,128)} %param.13) | copy-start | bytes 12292
  41.6 44.8 %copy-start.3 = (s32[8]{0:T(128)S(1)}, s32[8]{0:T(128)}, u32[]{:S(2)}) copy-start(s32[8]{0:T(128)} %param.11) | copy-start | bytes 100
  41.7 289.8 %all-reduce.2.cloned.1.call-start = ((), (), s32[]{:S(2)}) async-start(), calls=%async_computation.2 | async-start | bytes 131072 | tf_op jit(solution)/shard_map/psum | solution.py:54
Sparse Core Ops, SparseCore 0:
  41.8 43.4 reduce-scatter.1
  91.4 240.0 all-reduce.1
where the time goes:
time: 370 us
  waiting for transfers between devices  209 us (56%)
  blocking collectives  79.5 us (21%)
  other arithmetic  28.9 us (8%)
  matrix products  20 us (5%)
  between operations  14.2 us (4%)
  local copies, waits for them, and re-layouts  12.2 us (3%)
  starting transfers between devices  5.42 us (1%)
    psum x1, waiting for transfers between devices, shards(): gram, pull = lax.psum((gram_local, pull_local), ('tile', 'lev'))  161 us
    psum x1, blocking collectives, shards(): gram, pull = lax.psum((gram_local, pull_local), ('tile', 'lev'))  79.5 us
    reduce_scatter x1, waiting for transfers between devices, shards(): lax.psum_scatter(jnp.einsum('okij,okjm->oim', operator_blocks, chosen, pr...  41.4 us
    another operation x3, other arithmetic, shards(): lower = jnp.linalg.cholesky(identity + gram)  12.4 us
    another operation x2, other arithmetic, shards(): lax.linalg.triangular_solve(lower, identity, left_side=True, lower=True)  10.5 us
    dot_general x1, matrix products, shards(): jnp.einsum('okij,okjm->oim', operator_blocks, chosen, preferred_element_t...  10.1 us
    gather x1, local copies, waits for them, and re-layouts, shards(): chosen = column_blocks[flat_index]  8.62 us
  transfers between devices with their start and end apart: 4, of which 4 were waited for; matrix products, arithmetic and copies ran while one was open for 1% of the time, Pallas kernels for 0%

commit v1 on v0

--- a/solution.py
+++ b/solution.py
@@ -51,7 +51,12 @@
     gram_local = jnp.dot(spread.T, spread, precision=highest, preferred_element_type=jnp.float32)
     pull_local = jnp.dot(innovation, spread, precision=highest, preferred_element_type=jnp.float32)
     identity = jnp.eye(ensemble, dtype=jnp.float32)
-    gram, pull = lax.psum((gram_local, pull_local), ("tile", "lev"))
+
+    def group_zone_on(vals):
+        extra = lax.psum(vals, axis_name="lev")
+        return lax.psum(extra, axis_name="tile")
+
+    gram, pull = group_zone_on((gram_local, pull_local))
     lower = jnp.linalg.cholesky(identity + gram)
     inverse = lax.linalg.triangular_solve(lower, identity, left_side=True, lower=True)
     shift_weights = jnp.dot(inverse.T, jnp.dot(inverse, pull, precision=highest), precision=highest)

time: 370 us -> 334 us (0.903)
  waiting for transfers between devices: 209 us -> 174 us
  blocking collectives: 79.5 us -> 75.6 us
    psum x1 -> x2, waiting for transfers between devices: 161 us -> 126 us  [the longest x1 63.7 us: group_zone_on(): extra = lax.psum(vals, axis_name='lev')]
    psum x1 -> x2, blocking collectives: 79.5 us -> 75.6 us  [the longest x1 61.1 us: group_zone_on(): return lax.psum(extra, axis_name='tile')]
  transfers between devices with their start and end apart: 4 -> 5, of which waited for: 4 -> 5; matrix products, arithmetic and copies ran while one was open for 1% -> 1% of each run, Pallas kernels for 0% -> 0%
where the time goes in v1:
time: 334 us; the launch traced here: 331 us
  waiting for transfers between devices  174 us (52%)
  blocking collectives  75.6 us (23%)
  other arithmetic  28.9 us (9%)
  matrix products  20 us (6%)
  between operations  13.9 us (4%)
  local copies, waits for them, and re-layouts  12.2 us (4%)
  starting transfers between devices  5.46 us (2%)
    psum x1, waiting for transfers between devices, group_zone_on(): extra = lax.psum(vals, axis_name='lev')  63.7 us
    psum x1, waiting for transfers between devices, group_zone_on(): return lax.psum(extra, axis_name='tile')  62.8 us
    psum x1, blocking collectives, group_zone_on(): return lax.psum(extra, axis_name='tile')  61.1 us
    reduce_scatter x1, waiting for transfers between devices, shards(): lax.psum_scatter(jnp.einsum('okij,okjm->oim', operator_blocks, chosen, pr...  41.5 us
    psum x1, blocking collectives, group_zone_on(): extra = lax.psum(vals, axis_name='lev')  14.5 us
    another operation x3, other arithmetic, shards(): lower = jnp.linalg.cholesky(identity + gram)  12.4 us
    another operation x2, other arithmetic, shards(): lax.linalg.triangular_solve(lower, identity, left_side=True, lower=True)  10.5 us
    dot_general x1, matrix products, shards(): jnp.einsum('okij,okjm->oim', operator_blocks, chosen, preferred_element_t...  10.1 us
  transfers between devices with their start and end apart: 5, of which 5 were waited for; matrix products, arithmetic and copies ran while one was open for 1% of the time, Pallas kernels for 0%

profile of v1, /device:TPU:1, one launch (start us, length us, event | category | flops | bytes accessed | tf_op | source)
XLA Modules:
  0.0 330.6 jit_solution(8091747654081412660)
XLA Ops:
  7.2 0.0 reduce-scatter.2.cloned.1.call-start
  7.2 1.1 fusion.23
  8.3 4.0 %collective-permute-start = (bf16[4,256,128]{2,1,0:T(8,128)(2,1)S(1)}, bf16[4,256,128]{2,1,0:T(8,128)(2,1)S(1)}, u32[]{:S(2)}, u32[]{:S(2)}) collective-permute-start(bf16[4,256,128]{2,1,0:T(8,128)(2,1)S(1)} %get-tuple-element.6), channel_id=1, source_target_pairs={{0,8},{8,16},{16,24},{24,32},{32,40},{40,48},{48,56},{56,64},{64,7... | collective-permute-start | bytes 786440 | tf_op jit(solution)/shard_map/ppermute | solution.py:17
  12.3 1.3 collective-permute-start.1
  13.6 0.7 compare_select_fusion
  14.3 0.1 copy.14
  14.4 0.1 reshape.63
  14.6 2.7 collective-permute-done
  17.3 3.8 %collective-permute-done.1 = bf16[4,256,128]{2,1,0:T(8,128)(2,1)S(1)} collective-permute-done((bf16[4,256,128]{2,1,0:T(8,128)(2,1)S(1)}, bf16[4,256,128]{2,1,0:T(8,128)(2,1)S(1)}, u32[]{:S(2)}, u32[]{:S(2)}) %collective-permute-start.1) | collective-permute-done | bytes 262176 | tf_op jit(solution)/shard_map/ppermute | solution.py:18
  21.1 1.8 pad_maximum_fusion
  22.9 8.6 %gather_fusion = bf16[256,128,128]{2,1,0:T(8,128)(2,1)} fusion(bf16[80,128,128]{2,1,0:T(8,128)(2,1)S(1)} %bitcast.54, s32[1024]{0:T(1024)S(1)} %pad_clamp_fusion), kind=kCustom, calls=%fused_computation | custom fusion | bytes 16778240 | tf_op jit(solution)/shard_map/gather | solution.py:39
  31.5 10.1 %fusion.3 = f32[64,128,128]{1,2,0:T(8,128)} fusion(bf16[64,4,128,128]{3,2,1,0:T(8,128)(2,1)} %bitcast.55, bf16[1,64,4,128,128]{4,3,2,1,0:T(8,128)(2,1)} %param.8), kind=kOutput, calls=%fused_computation.8 | convolution fusion | flops 1073741824 | bytes 20971520 | tf_op jit(solution)/shard_map/okij,okjm->oim/dot_general | solution.py:41
  41.6 0.0 copy-start
  41.6 0.0 copy-start.1
  41.6 0.0 copy-start.2
  41.6 0.0 copy-start.3
  41.6 0.0 reduce-scatter.2.cloned.1.call-update
  41.7 0.0 all-reduce.3.cloned.1.call-start
  41.7 1.5 copy-done
  43.2 0.6 convert_reduce_fusion
  43.9 41.5 %reduce-scatter.2.cloned.1.call-done = f32[8,128,128]{1,2,0:T(8,128)} async-done(((f32[64,128,128]{1,2,0:T(8,128)}), f32[8,128,128]{1,2,0:T(8,128)}) %reduce-scatter.2.cloned.1.call-update) | async-done | bytes 524304 | tf_op jit(solution)/shard_map/reduce_scatter | solution.py:40
  85.3 1.1 reduce_sum.19
  86.4 0.0 copy-done.1
  86.4 0.0 copy-done.2
  86.4 0.0 copy-done.3
  86.4 0.1 subtract_multiply_fusion.3
  86.5 2.5 convolution_bitcast_fusion
  89.0 0.0 all-reduce.3.cloned.1.call-update
  89.0 0.0 all-reduce.5.cloned.1.call-start
  89.1 63.7 %all-reduce.3.cloned.1.call-done = f32[128,128]{1,0:T(8,128)} async-done(((f32[128,128]{1,0:T(8,128)}), f32[128,128]{1,0:T(8,128)}) %all-reduce.3.cloned.1.call-update) | async-done | bytes 65552 | tf_op jit(solution)/shard_map/psum | solution.py:56
  152.7 0.0 all-reduce.5.cloned.1.call-update
  152.8 1.6 convolution_bitcast_fusion.3
  154.3 14.5 %psum.30 = f32[128]{0:T(128)S(1)} all-reduce(f32[128]{0:T(128)S(1)} %convolution_bitcast_fusion.3), channel_id=1, replica_groups=mesh['tile'=32,'lev'=8] {'lev'}, use_global_device_ids=true, to_apply=%region_7.8 | all-reduce | flops 128 | bytes 1024 | tf_op jit(solution)/shard_map/psum | solution.py:56
  168.8 61.1 %psum.31 = f32[128]{0:T(128)S(1)} all-reduce(f32[128]{0:T(128)S(1)} %psum.30), channel_id=1, replica_groups=mesh['tile'=32,'lev'=8] {'tile'}, use_global_device_ids=true, to_apply=%region_8.9 | all-reduce | flops 128 | bytes 1024 | tf_op jit(solution)/shard_map/psum | solution.py:57
  229.9 62.8 %all-reduce.5.cloned.1.call-done = f32[128,128]{1,0:T(8,128)} async-done(((f32[128,128]{1,0:T(8,128)}), f32[128,128]{1,0:T(8,128)}) %all-reduce.5.cloned.1.call-update) | async-done | bytes 65552 | tf_op jit(solution)/shard_map/psum | solution.py:57
  292.7 0.9 convert_add_fusion
  293.5 0.1 copy.17
  293.6 0.9 fusion.17
  294.5 11.7 %cholesky.18 = f32[128,128]{1,0:T(8,128)S(1)} custom-call(f32[128,128]{1,0:T(8,128)S(1)} %fusion.17), custom_call_target="Cholesky" | custom-call | tf_op jit(solution)/shard_map/jit(cholesky)/cholesky | solution.py:60
  306.3 0.6 compare_reduce_fusion
  306.9 0.7 fusion.13
  307.6 9.8 %custom-call.6 = f32[1,128,128]{1,2,0:T(8,128)S(1)} custom-call(f32[1,128,128]{2,1,0:T(8,128)S(1)} %fusion.13), custom_call_target="InvertDiagBlocksLowerTriangular" | custom-call | tf_op jit(solution)/shard_map/triangular_solve | solution.py:61
  317.4 0.2 fusion.15
  317.6 0.2 convolution_bitcast_fusion.2
  317.8 0.2 fusion.8
  318.0 0.7 copy.19
  318.8 5.3 %add_convert_fusion = bf16[4,2048,128]{2,1,0:T(8,128)(2,1)} fusion(bf16[4,2048,128]{2,1,0:T(8,128)(2,1)S(1)} %copy-done, f32[4,2048]{1,0:T(4,128)S(1)} %broadcast_multiply_fusion, f32[128,128]{0,1:T(8,128)S(1)} %bitcast_add_fusion), kind=kOutput, calls=%fused_computation.6 | convolution fusion | flops 273694720 | bytes 4292608 | tf_op jit(solution)/shard_map/dot_general | solution.py:67
  (4 shorter events, 0.1 us)
Async XLA Ops:
  7.2 78.2 %reduce-scatter.2.cloned.1.call-start = ((), (), s32[]{:S(2)}) async-start(), calls=%async_computation.1 | async-start | bytes 4718592 | tf_op jit(solution)/shard_map/reduce_scatter | solution.py:40
  8.3 9.0 %collective-permute-start = (bf16[4,256,128]{2,1,0:T(8,128)(2,1)S(1)}, bf16[4,256,128]{2,1,0:T(8,128)(2,1)S(1)}, u32[]{:S(2)}, u32[]{:S(2)}) collective-permute-start(bf16[4,256,128]{2,1,0:T(8,128)(2,1)S(1)} %get-tuple-element.6), channel_id=1, source_target_pairs={{0,8},{8,16},{16,24},{24,32},{32,40},{40,48},{48,56},{56,64},{64,7... | collective-permute-start | bytes 786440 | tf_op jit(solution)/shard_map/ppermute | solution.py:17
  12.3 8.8 %collective-permute-start.1 = (bf16[4,256,128]{2,1,0:T(8,128)(2,1)S(1)}, bf16[4,256,128]{2,1,0:T(8,128)(2,1)S(1)}, u32[]{:S(2)}, u32[]{:S(2)}) collective-permute-start(bf16[4,256,128]{2,1,0:T(8,128)(2,1)S(1)} %get-tuple-element.7), channel_id=1, source_target_pairs={{8,0},{16,8},{24,16},{32,24},{40,32},{48,40},{56,48},{64,56},{72,6... | collective-permute-start | bytes 786440 | tf_op jit(solution)/shard_map/ppermute | solution.py:18
  41.6 1.6 copy-start
  41.6 44.8 %copy-start.1 = (f32[8,128]{1,0:T(8,128)S(1)}, f32[8,128]{1,0:T(8,128)}, u32[]{:S(2)}) copy-start(f32[8,128]{1,0:T(8,128)} %param.12) | copy-start | bytes 12292
  41.6 44.8 %copy-start.2 = (f32[8,128]{1,0:T(8,128)S(1)}, f32[8,128]{1,0:T(8,128)}, u32[]{:S(2)}) copy-start(f32[8,128]{1,0:T(8,128)} %param.13) | copy-start | bytes 12292
  41.6 44.8 %copy-start.3 = (s32[8]{0:T(128)S(1)}, s32[8]{0:T(128)}, u32[]{:S(2)}) copy-start(s32[8]{0:T(128)} %param.11) | copy-start | bytes 100
  41.7 111.1 %all-reduce.3.cloned.1.call-start = ((), (), s32[]{:S(2)}) async-start(), calls=%async_computation.2 | async-start | bytes 131072 | tf_op jit(solution)/shard_map/psum | solution.py:56
  89.0 203.7 %all-reduce.5.cloned.1.call-start = ((), (), s32[]{:S(2)}) async-start(), calls=%async_computation.3 | async-start | bytes 131072 | tf_op jit(solution)/shard_map/psum | solution.py:57
Sparse Core Ops, SparseCore 0:
  41.8 43.4 reduce-scatter.1
  89.1 63.5 all-reduce.2
  156.6 136.0 all-reduce.4
